TPU v7x, 32 devices: a whole 2x2x4 slice. The times are simulated.
32 devices in a mesh: head: 2 (over core), blk: 16 (over z, y, x).
Axes of the slice: x: 2, y: 2, z: 4, core: 2. Of those that a mesh axis runs over, the one named last changes fastest.
Arguments:
- doc_x: bfloat16 [8192, 1024], P('blk'), may hold values from -27 to 27
- doc_query: bfloat16 [8192, 1024], P('blk', 'head'), may hold values from -36 to 36
- doc_key: bfloat16 [8192, 1024], P('blk', 'head'), may hold values from -36 to 36
- doc_value: bfloat16 [8192, 1024], P('blk', 'head'), may hold values from -8 to 8
- key_cache: bfloat16 [256, 16, 1024], P('blk', None, 'head'), may hold values from -9 to 9
- value_cache: bfloat16 [256, 16, 1024], P('blk', None, 'head'), may hold values from -8 to 8
- rel_embed: bfloat16 [512, 1024], replicated, may hold values from -6 to 6
- w_query: bfloat16 [1024, 1024], P(None, 'head'), may hold values from -0.1875 to 0.1875
- w_key: bfloat16 [1024, 1024], P(None, 'head'), may hold values from -0.1875 to 0.1875
- out_weight: bfloat16 [1024, 1024], P('head'), may hold values from -0.1875 to 0.1875
- ln_gain: float32 [1024], replicated, may hold values from 0.5 to 1.5
- ln_bias: float32 [1024], replicated, may hold values from -3 to 3
- score_weight: float32 [1024], replicated, may hold values from -0.1875 to 0.1875
- query_len: int32 [4], replicated, may hold values from 1 to 1024, as said below
- dev_query: int32 [16], replicated, may hold values from 0 to 3, as said below
- page_table: int32 [4, 64], replicated, may hold values from 0 to 255, as said below
- tile_kind: int32 [32], P('blk'), may hold values 0 or 1
- rel_bucket: int32 [511], replicated, may hold values from 1 to 511, as said below
Outputs:
- normed: bfloat16 [8192, 1024], P('blk', 'head')
- segment_scores: float32 [512], P('blk')
Inputs may be any that keep to these rules, and one draw needn't show every extreme that they name: `query_len`: one query has exactly 1024 tokens. `dev_query`: each query is named by exactly 4 entries. `page_table`: a permutation of the 256 cache pages; the pages of one index of blk belong to 4 different queries, 4 page each. `rel_bucket`: entry 255 + d is the bucket of distance d; nondecreasing in d; 256 at d = 0; d = 1 and d = 2 share the next bucket above, d = -1 and d = -2 the next below.
All inputs are finite; a program needn't handle non-finite values. No bound on the sum of `tile_kind` on one device may be relied on, other than what follows from the above.
Results may differ from a plain program's by a relative error of at most 0.0075.
Values may be sent and summed in bfloat16 or wider, within the bound.
A program may use at most 192 MiB of HBM per device.

v0:
```python
import functools

import jax
import jax.numpy as jnp
from jax import lax
from jax.experimental import pallas as pl
from jax.experimental.pallas import tpu as pltpu
from jax.sharding import PartitionSpec as P

HD = 64
DOCLEN = 256
SHORT = 16
MESH = pl.DeviceIdType.MESH
F32 = jnp.float32
BF16 = jnp.bfloat16
NEG = float("-inf")


def dot_t(a, b):
    return lax.dot_general(a, b, (((1,), (1,)), ((), ())), preferred_element_type=F32)


def skew(table):
    return pltpu.roll(table, 0, 1, stride=1, stride_axis=0)[:, DOCLEN:]


def kernel(
    n,
    slots,
    index_ref,
    kind_ref,
    keyc_ref,
    valuec_ref,
    embed_ref,
    wk_ref,
    wq_ref,
    bucket_ref,
    bias_ref,
    q_ref,
    k_ref,
    v_ref,
    ow_ref,
    x_ref,
    gain_ref,
    lnb_ref,
    sw_ref,
    out_ref,
    seg_ref,
    send_k,
    send_v,
    recv_k,
    recv_v,
    key_rel,
    query_rel,
    own,
    probs,
    att,
    part,
    other,
    hidden,
    send_sem,
    recv_sem,
    pair_send,
    pair_recv,
):
    me = lax.axis_index("blk")
    head = lax.axis_index("head")
    page = keyc_ref.shape[1]
    block = slots * page
    rows, cols = q_ref.shape
    tiles = rows // DOCLEN
    pairs = cols // (2 * HD)
    model = x_ref.shape[1]
    tokens = recv_k.shape[0]
    factor = float(1.4426950408889634 / (3.0 * HD) ** 0.5)

    barrier = pltpu.get_barrier_semaphore()

    def greet(step, carry):
        pl.semaphore_signal(
            barrier, inc=1, device_id={"blk": lax.rem(me + step, n)}, device_id_type=MESH
        )
        return carry

    lax.fori_loop(1, n, greet, 0)
    pl.semaphore_signal(barrier, inc=1, device_id={"head": 1 - head}, device_id_type=MESH)

    def pack(source, packed, dest):
        for slot in range(slots):
            packed[pl.ds(pl.multiple_of(dest * block + slot * page, page), page), :] = source[
                index_ref[dest * slots + slot]
            ]

    def pack_all(dest, carry):
        pack(keyc_ref, send_k, dest)
        pack(valuec_ref, send_v, dest)
        return carry

    lax.fori_loop(0, n, pack_all, 0)
    pl.semaphore_wait(barrier, n)

    def transfer(packed, landing, which, step):
        dest = lax.rem(me + step, n)
        return pltpu.make_async_remote_copy(
            src_ref=packed.at[pl.ds(pl.multiple_of(dest * block, block), block)],
            dst_ref=landing.at[pl.ds(pl.multiple_of(me * block, block), block)],
            send_sem=send_sem.at[which, step],
            recv_sem=recv_sem.at[which, step],
            device_id={"blk": dest},
            device_id_type=MESH,
        )

    def start_k(step, carry):
        transfer(send_k, recv_k, 0, step).start()
        return carry

    def start_v(step, carry):
        transfer(send_v, recv_v, 1, step).start()
        return carry

    lax.fori_loop(1, n, start_k, 0)
    lax.fori_loop(1, n, start_v, 0)
    mine = pl.ds(pl.multiple_of(me * block, block), block)
    recv_k[mine, :] = send_k[mine, :]
    recv_v[mine, :] = send_v[mine, :]

    picker = (
        bucket_ref[...] == lax.broadcasted_iota(jnp.int32, (2 * DOCLEN, embed_ref.shape[0]), 1)
    ).astype(BF16)
    for weight, table in ((wk_ref, key_rel), (wq_ref, query_rel)):
        projected = jnp.dot(embed_ref[...], weight[...], preferred_element_type=F32).astype(BF16)
        table[...] = jnp.dot(picker, projected, preferred_element_type=F32).astype(BF16)

    lane = lax.broadcasted_iota(jnp.int32, (1, 2 * HD), 1)
    halves = (lane < HD, lane >= HD)
    same_short = (
        lax.broadcasted_iota(jnp.int32, (DOCLEN, DOCLEN), 0) // SHORT
        == lax.broadcasted_iota(jnp.int32, (DOCLEN, DOCLEN), 1) // SHORT
    )

    def place(step):
        tile, pair = step // pairs, step % pairs
        tile_rows = pl.ds(pl.multiple_of(tile * DOCLEN, DOCLEN), DOCLEN)
        pair_cols = pl.ds(pl.multiple_of(pair * 2 * HD, 2 * HD), 2 * HD)
        return tile, tile_rows, pair_cols

    def own_scores(step, carry):
        tile, tile_rows, pair_cols = place(step)
        q = q_ref[tile_rows, pair_cols]
        k = k_ref[tile_rows, pair_cols]
        kr = key_rel[:, pair_cols]
        qr = query_rel[:, pair_cols]
        allowed = jnp.where(same_short, 1, kind_ref[tile]) == 1
        for half in range(2):
            qh = jnp.where(halves[half], q, jnp.zeros_like(q))
            kh = jnp.where(halves[half], k, jnp.zeros_like(k))
            scores = dot_t(qh, k) + skew(dot_t(qh, kr)) + skew(dot_t(kh, qr)).T
            own[step * 2 + half] = jnp.where(allowed, scores, NEG)
        return carry

    lax.fori_loop(0, tiles * pairs, own_scores, 0)

    def land_k(step, carry):
        transfer(send_k, recv_k, 0, step).wait_recv()
        return carry

    lax.fori_loop(1, n, land_k, 0)

    def weigh(step, carry):
        tile, tile_rows, pair_cols = place(step)
        q = q_ref[tile_rows, pair_cols]
        keys = recv_k[:, pair_cols]
        for half in range(2):
            qh = jnp.where(halves[half], q, jnp.zeros_like(q))
            cross = dot_t(qh, keys) + bias_ref[...]
            inner = own[step * 2 + half]
            top = jnp.maximum(
                jnp.max(cross, axis=1, keepdims=True), jnp.max(inner, axis=1, keepdims=True)
            )
            probs[step * 2 + half, :, :tokens] = jnp.exp2((cross - top) * factor).astype(BF16)
            probs[step * 2 + half, :, tokens:] = jnp.exp2((inner - top) * factor).astype(BF16)
        return carry

    lax.fori_loop(0, tiles * pairs, weigh, 0)

    def land_v(step, carry):
        transfer(send_v, recv_v, 1, step).wait_recv()
        return carry

    lax.fori_loop(1, n, land_v, 0)

    def gather_values(step, carry):
        tile, tile_rows, pair_cols = place(step)
        values = recv_v[:, pair_cols]
        inner = v_ref[tile_rows, pair_cols]
        sums = []
        for half in range(2):
            weights = probs[step * 2 + half]
            sums.append(
                jnp.dot(
                    weights[:, :tokens],
                    jnp.where(halves[half], values, jnp.ones_like(values)),
                    preferred_element_type=F32,
                )
                + jnp.dot(
                    weights[:, tokens:],
                    jnp.where(halves[half], inner, jnp.ones_like(inner)),
                    preferred_element_type=F32,
                )
            )
        top = jnp.where(halves[0], sums[0], sums[1])
        below = pltpu.roll(jnp.where(halves[0], sums[1], sums[0]), HD, 1)
        att[tile_rows, pair_cols] = (top / below).astype(BF16)
        return carry

    def swap(tile):
        return pltpu.make_async_remote_copy(
            src_ref=part.at[tile],
            dst_ref=other.at[tile],
            send_sem=pair_send.at[tile],
            recv_sem=pair_recv.at[tile],
            device_id={"head": 1 - head},
            device_id_type=MESH,
        )

    for tile in range(tiles):
        lax.fori_loop(tile * pairs, (tile + 1) * pairs, gather_values, 0)
        part[tile] = jnp.dot(
            att[tile * DOCLEN : (tile + 1) * DOCLEN, :], ow_ref[...], preferred_element_type=F32
        ).astype(BF16)
        swap(tile).start()

    here = pl.ds(pl.multiple_of(head * (model // 2), model // 2), model // 2)
    for tile in range(tiles):
        span = slice(tile * DOCLEN, (tile + 1) * DOCLEN)
        swap(tile).wait_recv()
        total = (
            x_ref[span, :].astype(F32) + part[tile].astype(F32) + other[tile].astype(F32)
        )
        mean = jnp.mean(total, axis=1, keepdims=True)
        centred = total - mean
        spread = jnp.mean(centred * centred, axis=1, keepdims=True)
        hidden[...] = centred * lax.rsqrt(spread + 1e-07)
        out_ref[span, :] = (
            hidden[:, here] * gain_ref[:, here] + lnb_ref[:, here]
        ).astype(BF16)
        firsts = jnp.concatenate(
            [hidden[row : row + 1, :] for row in range(0, DOCLEN, SHORT)], axis=0
        )
        full = firsts * gain_ref[...] + lnb_ref[...]
        seg_ref[tile * (DOCLEN // SHORT) : (tile + 1) * (DOCLEN // SHORT), :] = jnp.sum(
            full * sw_ref[...], axis=1, keepdims=True
        )

    def drain(step, carry):
        transfer(send_k, recv_k, 0, step).wait_send()
        transfer(send_v, recv_v, 1, step).wait_send()
        return carry

    lax.fori_loop(1, n, drain, 0)
    for tile in range(tiles):
        swap(tile).wait_send()


def shards(
    n,
    doc_x,
    doc_query,
    doc_key,
    doc_value,
    key_cache,
    value_cache,
    rel_embed,
    w_query,
    w_key,
    out_weight,
    ln_gain,
    ln_bias,
    score_weight,
    query_len,
    dev_query,
    page_table,
    tile_kind,
    rel_bucket,
):
    pages_here, page, cols = key_cache.shape
    queries, query_pages = page_table.shape
    slots = pages_here // queries
    tokens = query_pages * page
    rows, model = doc_x.shape
    tiles = rows // DOCLEN
    heads_here = cols // HD
    me = lax.axis_index("blk")

    rank = jnp.sum(
        (page_table[:, None, :] < page_table[:, :, None]).astype(jnp.int32), axis=2
    )
    wanted_rank = me * slots + jnp.arange(slots, dtype=jnp.int32)
    local = jnp.sum(
        jnp.where(rank[:, None, :] == wanted_rank[None, :, None], page_table[:, None, :], 0),
        axis=2,
    ) - me * pages_here
    names = dev_query[:, None] == jnp.arange(queries, dtype=jnp.int32)[None, :]
    index = jnp.sum(jnp.where(names[:, :, None], local[None], 0), axis=1).reshape(-1)
    my_query = dev_query[me]
    my_rank = rank[my_query]
    order = jnp.arange(query_pages, dtype=jnp.int32)
    page_of = jnp.sum(jnp.where(my_rank[None, :] == order[:, None], order[None, :], 0), axis=1)
    token = page_of[:, None] * page + jnp.arange(page, dtype=jnp.int32)[None, :]
    bias = jnp.where(token < query_len[my_query], 0.0, NEG).astype(F32).reshape(1, tokens)
    bucket = jnp.concatenate([jnp.full((1,), -1, jnp.int32), rel_bucket[::-1]])[:, None]

    vmem = pl.BlockSpec(memory_space=pltpu.VMEM)
    smem = pl.BlockSpec(memory_space=pltpu.SMEM)
    normed, seg = pl.pallas_call(
        functools.partial(kernel, n, slots),
        out_shape=(
            jax.ShapeDtypeStruct((rows, model // 2), BF16),
            jax.ShapeDtypeStruct((rows // SHORT, 1), F32),
        ),
        in_specs=[smem, smem] + [vmem] * 15,
        out_specs=(vmem, vmem),
        scratch_shapes=[
            pltpu.VMEM((n * slots * page, cols), BF16),
            pltpu.VMEM((n * slots * page, cols), BF16),
            pltpu.VMEM((tokens, cols), BF16),
            pltpu.VMEM((tokens, cols), BF16),
            pltpu.VMEM((2 * DOCLEN, cols), BF16),
            pltpu.VMEM((2 * DOCLEN, cols), BF16),
            pltpu.VMEM((tiles * heads_here, DOCLEN, DOCLEN), F32),
            pltpu.VMEM((tiles * heads_here, DOCLEN, tokens + DOCLEN), BF16),
            pltpu.VMEM((rows, cols), BF16),
            pltpu.VMEM((tiles, DOCLEN, model), BF16),
            pltpu.VMEM((tiles, DOCLEN, model), BF16),
            pltpu.VMEM((DOCLEN, model), F32),
            pltpu.SemaphoreType.DMA((2, n)),
            pltpu.SemaphoreType.DMA((2, n)),
            pltpu.SemaphoreType.DMA((tiles,)),
            pltpu.SemaphoreType.DMA((tiles,)),
        ],
        compiler_params=pltpu.CompilerParams(
            collective_id=0, has_side_effects=True, vmem_limit_bytes=56 * 1024 * 1024
        ),
        cost_estimate=pl.CostEstimate(
            flops=8_000_000_000, bytes_accessed=12_000_000, transcendentals=5_000_000
        ),
    )(
        index,
        tile_kind,
        key_cache,
        value_cache,
        rel_embed,
        w_key,
        w_query,
        bucket,
        bias,
        doc_query,
        doc_key,
        doc_value,
        out_weight,
        doc_x,
        ln_gain[None, :],
        ln_bias[None, :],
        score_weight[None, :],
    )
    return normed, seg.reshape(-1)


def solution(mesh):
    in_specs = (
        P("blk", None),
        P("blk", "head"),
        P("blk", "head"),
        P("blk", "head"),
        P("blk", None, "head"),
        P("blk", None, "head"),
        P(),
        P(None, "head"),
        P(None, "head"),
        P("head", None),
        P(),
        P(),
        P(),
        P(),
        P(),
        P(),
        P("blk"),
        P(),
    )
    out_specs = (P("blk", "head"), P("blk"))
    return jax.shard_map(
        functools.partial(shards, mesh.shape["blk"]),
        mesh=mesh,
        in_specs=in_specs,
        out_specs=out_specs,
        check_vma=False,
    )
```

profile of v0, /device:TPU:15, one launch (start us, length us, event | category | flops | bytes accessed | tf_op | source)
XLA Modules:
  0.0 77.5 jit_solution(4057280293551111684)
XLA Ops:
  0.6 0.0 copy-start.3
  0.6 0.6 copy-done.3
  1.3 0.6 dynamic_slice.9
  3.8 0.0 copy-start.2
  3.8 0.6 copy-done.2
  4.5 0.6 dynamic_slice.11
  5.1 0.0 copy-start
  5.1 0.7 copy-done
  5.8 0.2 convert_reduce_fusion
  6.0 0.2 select_reduce_fusion.2
  6.2 0.1 select_reduce_fusion.1
  6.3 0.0 copy-start.1
  6.3 0.1 select_reduce_fusion
  6.4 0.6 copy-done.1
  7.0 0.1 reverse
  7.1 0.1 slice
  7.2 0.1 pad_add_fusion
  7.2 0.1 copy.21
  7.3 0.6 reshape.79.index_ref
  7.9 0.7 fusion
  8.6 0.7 select_n.39.bias_ref
  9.3 0.9 %copy.22.bucket_ref = s32[512,1]{1,0:T(8,128)} copy(s32[512,1]{0,1:T(1,128)S(1)} %bitcast.9) | data formatting | bytes 4096 | tf_op jit(solution)/shard_map/broadcast_in_dim | solution.py:311
  10.2 64.1 %shard_map.185 = (bf16[512,512]{1,0:T(8,128)(2,1)}, f32[32,1]{1,0:T(8,128)}) custom-call(s32[64]{0:T(128)} %reshape.79.index_ref, s32[2]{0:T(128)} %kind_ref.1, bf16[16,16,512]{2,1,0:T(8,128)(2,1)} %keyc_ref.1, bf16[16,16,512]{2,1,0:T(8,128)(2,1)} %valuec_ref.1, bf16[512,1024]{1,0:T(8,128)(2,1)} %embed_ref.1, bf16[1024,512]{1,0:T(8,128)(2,1)} %wk_ref.1, ...), custom_call_target="tpu_custom_call" | custom-call | flops 8000000000 | bytes 12000000 | tf_op jit(solution)/shard_map/pallas_call | solution.py:315
  74.3 1.3 %reduce = f32[32]{0:T(128)} reduce(f32[32,1]{1,0:T(8,128)} %get-tuple-element.5, f32[]{:T(128)} %constant.18), dimensions={1}, to_apply=%get-tuple-element.5.reduce_sub_computation | reduce | bytes 260 | tf_op jit(solution)/shard_map/pallas_call | solution.py:315
  75.6 1.9 %copy.24 = bf16[512,512]{1,0:T(8,128)(2,1)} copy(bf16[512,512]{1,0:T(8,128)(2,1)} %get-tuple-element.8) | data formatting | bytes 1048576
  (5 shorter events, 0.0 us)
Async XLA Ops:
  0.6 0.7 copy-start.3
  3.8 0.7 copy-start.2
  5.1 0.7 copy-start
  6.3 0.7 copy-start.1
where the time goes:
time: 77.8 us; the launch traced here: 77.5 us
  Pallas kernels  64.1 us (82%)
  local copies, waits for them, and re-layouts  7.97 us (10%)
  other arithmetic  2.78 us (4%)
  between operations  2.65 us (3%)
    pallas_call x1, Pallas kernels, shards(): pl.pallas_call(functools.partial(kernel, n, slots), out_shape=(jax.ShapeD...  64.1 us
    unnamed x11, local copies, waits for them, and re-layouts  4.57 us

commit v1 on v0

--- a/solution.py
+++ b/solution.py
@@ -26,26 +26,36 @@
 
 def kernel(
     n,
-    slots,
-    index_ref,
     kind_ref,
+    asked_ref,
+    length_ref,
+    table_ref,
     keyc_ref,
     valuec_ref,
+    bucket_ref,
+    gain_ref,
+    lnb_ref,
+    sw_ref,
+    embed_hbm,
+    wk_hbm,
+    wq_hbm,
+    q_hbm,
+    k_hbm,
+    v_hbm,
+    ow_hbm,
+    x_hbm,
+    out_ref,
+    seg_ref,
     embed_ref,
     wk_ref,
     wq_ref,
-    bucket_ref,
-    bias_ref,
     q_ref,
     k_ref,
     v_ref,
     ow_ref,
     x_ref,
-    gain_ref,
-    lnb_ref,
-    sw_ref,
-    out_ref,
-    seg_ref,
+    sorted_k,
+    sorted_v,
     send_k,
     send_v,
     recv_k,
@@ -58,6 +68,7 @@
     part,
     other,
     hidden,
+    load_sem,
     send_sem,
     recv_sem,
     pair_send,
@@ -65,13 +76,15 @@
 ):
     me = lax.axis_index("blk")
     head = lax.axis_index("head")
-    page = keyc_ref.shape[1]
-    block = slots * page
-    rows, cols = q_ref.shape
+    pages_here, page, cols = keyc_ref.shape
+    queries, query_pages = table_ref.shape
+    block = pages_here // queries * page
+    rows = q_ref.shape[0]
     tiles = rows // DOCLEN
     pairs = cols // (2 * HD)
     model = x_ref.shape[1]
     tokens = recv_k.shape[0]
+    local = pages_here * page
     factor = float(1.4426950408889634 / (3.0 * HD) ** 0.5)
 
     barrier = pltpu.get_barrier_semaphore()
@@ -85,18 +98,62 @@
     lax.fori_loop(1, n, greet, 0)
     pl.semaphore_signal(barrier, inc=1, device_id={"head": 1 - head}, device_id_type=MESH)
 
-    def pack(source, packed, dest):
-        for slot in range(slots):
-            packed[pl.ds(pl.multiple_of(dest * block + slot * page, page), page), :] = source[
-                index_ref[dest * slots + slot]
-            ]
-
-    def pack_all(dest, carry):
-        pack(keyc_ref, send_k, dest)
-        pack(valuec_ref, send_v, dest)
-        return carry
-
-    lax.fori_loop(0, n, pack_all, 0)
+    loads = [
+        pltpu.make_async_copy(source, target, load_sem.at[place])
+        for place, (source, target) in enumerate(
+            (
+                (embed_hbm, embed_ref),
+                (wk_hbm, wk_ref),
+                (wq_hbm, wq_ref),
+                (q_hbm, q_ref),
+                (k_hbm, k_ref),
+                (v_hbm, v_ref),
+                (ow_hbm, ow_ref),
+                (x_hbm, x_ref),
+            )
+        )
+    ]
+    for load in loads:
+        load.start()
+
+    def iota(shape, axis):
+        return lax.broadcasted_iota(jnp.int32, shape, axis)
+
+    square = (query_pages, query_pages)
+    diagonal = iota(square, 0) == iota(square, 1)
+
+    def upright(line):
+        return jnp.sum(jnp.where(diagonal, line, 0), axis=1, keepdims=True)
+
+    token = iota((1, local), 1)
+    first = me * pages_here
+    page_id = first + token // page
+    target = jnp.zeros((1, local), jnp.int32)
+    for query in range(queries):
+        listed = upright(table_ref[query : query + 1, :])
+        hit = jnp.sum((listed == page_id).astype(jnp.int32), axis=0, keepdims=True)
+        before = jnp.sum(
+            jnp.logical_and(listed >= first, listed < page_id).astype(jnp.int32),
+            axis=0,
+            keepdims=True,
+        )
+        target = target + hit * (query * block + before * page)
+    target = target + token % page
+    order = (iota((local, local), 0) == target).astype(BF16)
+    for source, arranged in ((keyc_ref, sorted_k), (valuec_ref, sorted_v)):
+        arranged[...] = (
+            jnp.dot(order, source[...].reshape(local, cols), preferred_element_type=F32)
+            .astype(BF16)
+            .reshape(queries, block, cols)
+        )
+
+    def pack(dest, carry):
+        spot = pl.ds(pl.multiple_of(dest * block, block), block)
+        send_k[spot, :] = sorted_k[asked_ref[dest]]
+        send_v[spot, :] = sorted_v[asked_ref[dest]]
+        return carry
+
+    lax.fori_loop(0, n, pack, 0)
     pl.semaphore_wait(barrier, n)
 
     def transfer(packed, landing, which, step):
@@ -124,9 +181,29 @@
     recv_k[mine, :] = send_k[mine, :]
     recv_v[mine, :] = send_v[mine, :]
 
-    picker = (
-        bucket_ref[...] == lax.broadcasted_iota(jnp.int32, (2 * DOCLEN, embed_ref.shape[0]), 1)
-    ).astype(BF16)
+    my_query = asked_ref[me]
+    wanted = jnp.sum(
+        jnp.where(iota((queries, query_pages), 0) == my_query, table_ref[...], 0),
+        axis=0,
+        keepdims=True,
+    )
+    rank = jnp.sum((wanted < upright(wanted)).astype(jnp.int32), axis=1, keepdims=True)
+    spread_shape = (query_pages, tokens)
+    place_id = jnp.sum(
+        jnp.where(rank == iota(spread_shape, 1) // page, iota(spread_shape, 0), 0),
+        axis=0,
+        keepdims=True,
+    )
+    allowed_token = place_id * page + iota((1, tokens), 1) % page < length_ref[my_query]
+    bias = jnp.where(allowed_token, 0.0, NEG).astype(F32)
+
+    buckets = embed_ref.shape[0]
+    distances = bucket_ref.shape[1]
+    flipped = iota((2 * DOCLEN, distances), 0) + iota((2 * DOCLEN, distances), 1) == distances
+    bucket = jnp.sum(jnp.where(flipped, bucket_ref[...], 0), axis=1, keepdims=True)
+    for load in loads[:3]:
+        load.wait()
+    picker = (bucket == iota((2 * DOCLEN, buckets), 1)).astype(BF16)
     for weight, table in ((wk_ref, key_rel), (wq_ref, query_rel)):
         projected = jnp.dot(embed_ref[...], weight[...], preferred_element_type=F32).astype(BF16)
         table[...] = jnp.dot(picker, projected, preferred_element_type=F32).astype(BF16)
@@ -158,6 +235,8 @@
             own[step * 2 + half] = jnp.where(allowed, scores, NEG)
         return carry
 
+    for load in loads[3:]:
+        load.wait()
     lax.fori_loop(0, tiles * pairs, own_scores, 0)
 
     def land_k(step, carry):
@@ -172,7 +251,7 @@
         keys = recv_k[:, pair_cols]
         for half in range(2):
             qh = jnp.where(halves[half], q, jnp.zeros_like(q))
-            cross = dot_t(qh, keys) + bias_ref[...]
+            cross = dot_t(qh, keys) + bias
             inner = own[step * 2 + half]
             top = jnp.maximum(
                 jnp.max(cross, axis=1, keepdims=True), jnp.max(inner, axis=1, keepdims=True)
@@ -230,6 +309,7 @@
         ).astype(BF16)
         swap(tile).start()
 
+    seg_row = jnp.zeros(seg_ref.shape, F32)
     here = pl.ds(pl.multiple_of(head * (model // 2), model // 2), model // 2)
     for tile in range(tiles):
         span = slice(tile * DOCLEN, (tile + 1) * DOCLEN)
@@ -248,9 +328,12 @@
             [hidden[row : row + 1, :] for row in range(0, DOCLEN, SHORT)], axis=0
         )
         full = firsts * gain_ref[...] + lnb_ref[...]
-        seg_ref[tile * (DOCLEN // SHORT) : (tile + 1) * (DOCLEN // SHORT), :] = jnp.sum(
-            full * sw_ref[...], axis=1, keepdims=True
-        )
+        scores = jnp.sum(full * sw_ref[...], axis=1, keepdims=True)
+        segments = DOCLEN // SHORT
+        column = iota((segments, tiles * segments), 1) - tile * segments
+        spread_scores = jnp.where(iota((segments, tiles * segments), 0) == column, scores, 0.0)
+        seg_row = seg_row + jnp.sum(spread_scores, axis=0, keepdims=True)
+    seg_ref[...] = seg_row
 
     def drain(step, carry):
         transfer(send_k, recv_k, 0, step).wait_send()
@@ -285,44 +368,35 @@
 ):
     pages_here, page, cols = key_cache.shape
     queries, query_pages = page_table.shape
-    slots = pages_here // queries
     tokens = query_pages * page
+    block = pages_here // queries * page
     rows, model = doc_x.shape
     tiles = rows // DOCLEN
     heads_here = cols // HD
-    me = lax.axis_index("blk")
-
-    rank = jnp.sum(
-        (page_table[:, None, :] < page_table[:, :, None]).astype(jnp.int32), axis=2
-    )
-    wanted_rank = me * slots + jnp.arange(slots, dtype=jnp.int32)
-    local = jnp.sum(
-        jnp.where(rank[:, None, :] == wanted_rank[None, :, None], page_table[:, None, :], 0),
-        axis=2,
-    ) - me * pages_here
-    names = dev_query[:, None] == jnp.arange(queries, dtype=jnp.int32)[None, :]
-    index = jnp.sum(jnp.where(names[:, :, None], local[None], 0), axis=1).reshape(-1)
-    my_query = dev_query[me]
-    my_rank = rank[my_query]
-    order = jnp.arange(query_pages, dtype=jnp.int32)
-    page_of = jnp.sum(jnp.where(my_rank[None, :] == order[:, None], order[None, :], 0), axis=1)
-    token = page_of[:, None] * page + jnp.arange(page, dtype=jnp.int32)[None, :]
-    bias = jnp.where(token < query_len[my_query], 0.0, NEG).astype(F32).reshape(1, tokens)
-    bucket = jnp.concatenate([jnp.full((1,), -1, jnp.int32), rel_bucket[::-1]])[:, None]
 
     vmem = pl.BlockSpec(memory_space=pltpu.VMEM)
     smem = pl.BlockSpec(memory_space=pltpu.SMEM)
     normed, seg = pl.pallas_call(
-        functools.partial(kernel, n, slots),
+        functools.partial(kernel, n),
         out_shape=(
             jax.ShapeDtypeStruct((rows, model // 2), BF16),
-            jax.ShapeDtypeStruct((rows // SHORT, 1), F32),
+            jax.ShapeDtypeStruct((1, rows // SHORT), F32),
         ),
-        in_specs=[smem, smem] + [vmem] * 15,
+        in_specs=[smem] * 3 + [vmem] * 7 + [pl.BlockSpec(memory_space=pl.ANY)] * 8,
         out_specs=(vmem, vmem),
         scratch_shapes=[
-            pltpu.VMEM((n * slots * page, cols), BF16),
-            pltpu.VMEM((n * slots * page, cols), BF16),
+            pltpu.VMEM(rel_embed.shape, BF16),
+            pltpu.VMEM(w_key.shape, BF16),
+            pltpu.VMEM(w_query.shape, BF16),
+            pltpu.VMEM((rows, cols), BF16),
+            pltpu.VMEM((rows, cols), BF16),
+            pltpu.VMEM((rows, cols), BF16),
+            pltpu.VMEM(out_weight.shape, BF16),
+            pltpu.VMEM((rows, model), BF16),
+            pltpu.VMEM((queries, block, cols), BF16),
+            pltpu.VMEM((queries, block, cols), BF16),
+            pltpu.VMEM((n * block, cols), BF16),
+            pltpu.VMEM((n * block, cols), BF16),
             pltpu.VMEM((tokens, cols), BF16),
             pltpu.VMEM((tokens, cols), BF16),
             pltpu.VMEM((2 * DOCLEN, cols), BF16),
@@ -333,6 +407,7 @@
             pltpu.VMEM((tiles, DOCLEN, model), BF16),
             pltpu.VMEM((tiles, DOCLEN, model), BF16),
             pltpu.VMEM((DOCLEN, model), F32),
+            pltpu.SemaphoreType.DMA((8,)),
             pltpu.SemaphoreType.DMA((2, n)),
             pltpu.SemaphoreType.DMA((2, n)),
             pltpu.SemaphoreType.DMA((tiles,)),
@@ -345,23 +420,24 @@
             flops=8_000_000_000, bytes_accessed=12_000_000, transcendentals=5_000_000
         ),
     )(
-        index,
         tile_kind,
+        dev_query,
+        query_len,
+        page_table,
         key_cache,
         value_cache,
+        rel_bucket[None, :],
+        ln_gain[None, :],
+        ln_bias[None, :],
+        score_weight[None, :],
         rel_embed,
         w_key,
         w_query,
-        bucket,
-        bias,
         doc_query,
         doc_key,
         doc_value,
         out_weight,
         doc_x,
-        ln_gain[None, :],
-        ln_bias[None, :],
-        score_weight[None, :],
     )
     return normed, seg.reshape(-1)
 

time: 77.8 us -> 65.2 us (0.84)
  local copies, waits for them, and re-layouts: 7.97 us -> 2.38 us
  other arithmetic: 2.78 us -> 0 us
  Pallas kernels: 64.1 us -> 62 us
  between operations: 2.65 us -> 0.65 us
    unnamed x11 -> x4, local copies, waits for them, and re-layouts: 4.57 us -> 2.38 us
    pallas_call x1, Pallas kernels: 64.1 us -> 62 us  [shards(): pl.pallas_call(functools.partial(kernel, n), out_shape=(jax.ShapeDtypeStr...]
    pallas_call x1 -> x0, other arithmetic: 1.35 us -> none  [shards(): pl.pallas_call(functools.partial(kernel, n, slots), out_shape=(jax.ShapeD...]
    dynamic_slice x2 -> x0, local copies, waits for them, and re-layouts: 1.16 us -> none  [the longest x1 0.58 us: shards(): my_query = dev_query[me]]
    broadcast_in_dim x1 -> x0, local copies, waits for them, and re-layouts: 0.86 us -> none  [shards(): jnp.concatenate([jnp.full((1,), -1, jnp.int32), rel_bucket[::-1]])[:, None]]
where the time goes in v1:
time: 65.2 us; the launch traced here: 65.1 us
  Pallas kernels  62 us (95%)
  local copies, waits for them, and re-layouts  2.38 us (4%)
    pallas_call x1, Pallas kernels, shards(): pl.pallas_call(functools.partial(kernel, n), out_shape=(jax.ShapeDtypeStr...  62 us
    unnamed x4, local copies, waits for them, and re-layouts  2.38 us

profile of v1, /device:TPU:15, one launch (start us, length us, event | category | flops | bytes accessed | tf_op | source)
XLA Modules:
  0.0 65.1 jit_solution(18228633513423321135)
XLA Ops:
  0.6 62.0 %shard_map.185 = (bf16[512,512]{1,0:T(8,128)(2,1)}, f32[1,32]{1,0:T(1,128)}) custom-call(s32[2]{0:T(128)} %kind_ref.1, s32[16]{0:T(128)} %asked_ref.1, s32[4]{0:T(128)} %length_ref.1, s32[4,64]{1,0:T(4,128)} %table_ref.1, bf16[16,16,512]{2,1,0:T(8,128)(2,1)} %keyc_ref.1, bf16[16,16,512]{2,1,0:T(8,128)(2,1)} %valuec_ref.1, s32[1,511]{1,0:T(1,128)} %bitcast.8, ...), custom_call_target="tpu_custom_call" | custom-call | flops 8000000000 | bytes 12000000 | tf_op jit(solution)/shard_map/pallas_call | solution.py:379
  62.7 0.0 copy-start
  62.7 1.9 %copy.22 = bf16[512,512]{1,0:T(8,128)(2,1)} copy(bf16[512,512]{1,0:T(8,128)(2,1)} %get-tuple-element.8) | data formatting | bytes 1048576
  64.5 0.0 copy-done
  64.5 0.5 copy.23
Async XLA Ops:
  62.7 1.9 %copy-start = (f32[1,32]{1,0:T(1,128)S(1)}, f32[1,32]{1,0:T(1,128)}, u32[]{:S(2)}) copy-start(f32[1,32]{1,0:T(1,128)} %get-tuple-element.5) | copy-start | bytes 388

commit v2 on v1

--- a/solution.py
+++ b/solution.py
@@ -10,6 +10,7 @@
 HD = 64
 DOCLEN = 256
 SHORT = 16
+PLANES = 4
 MESH = pl.DeviceIdType.MESH
 F32 = jnp.float32
 BF16 = jnp.bfloat16
@@ -62,19 +63,25 @@
     recv_v,
     key_rel,
     query_rel,
-    own,
-    probs,
+    bias_ref,
+    top_ref,
+    acc,
     att,
     part,
     other,
     hidden,
     load_sem,
+    line_send,
+    line_recv,
     send_sem,
     recv_sem,
     pair_send,
     pair_recv,
+    *passing,
 ):
     me = lax.axis_index("blk")
+    width = n // PLANES
+    plane, column = me // width, lax.rem(me, width)
     head = lax.axis_index("head")
     pages_here, page, cols = keyc_ref.shape
     queries, query_pages = table_ref.shape
@@ -83,20 +90,31 @@
     tiles = rows // DOCLEN
     pairs = cols // (2 * HD)
     model = x_ref.shape[1]
-    tokens = recv_k.shape[0]
     local = pages_here * page
+    tokens = PLANES * local
     factor = float(1.4426950408889634 / (3.0 * HD) ** 0.5)
 
     barrier = pltpu.get_barrier_semaphore()
+
+    def in_plane(step):
+        return plane * width + lax.rem(column + step, width)
 
     def greet(step, carry):
         pl.semaphore_signal(
-            barrier, inc=1, device_id={"blk": lax.rem(me + step, n)}, device_id_type=MESH
+            barrier, inc=1, device_id={"blk": in_plane(step)}, device_id_type=MESH
         )
         return carry
 
-    lax.fori_loop(1, n, greet, 0)
+    lax.fori_loop(1, width, greet, 0)
     pl.semaphore_signal(barrier, inc=1, device_id={"head": 1 - head}, device_id_type=MESH)
+
+    @pl.when(plane > 0)
+    def _():
+        pl.semaphore_signal(barrier, inc=1, device_id={"blk": me - width}, device_id_type=MESH)
+
+    @pl.when(plane < PLANES - 1)
+    def _():
+        pl.semaphore_signal(barrier, inc=1, device_id={"blk": me + width}, device_id_type=MESH)
 
     loads = [
         pltpu.make_async_copy(source, target, load_sem.at[place])
@@ -147,39 +165,81 @@
             .reshape(queries, block, cols)
         )
 
-    def pack(dest, carry):
-        spot = pl.ds(pl.multiple_of(dest * block, block), block)
-        send_k[spot, :] = sorted_k[asked_ref[dest]]
-        send_v[spot, :] = sorted_v[asked_ref[dest]]
-        return carry
-
-    lax.fori_loop(0, n, pack, 0)
-    pl.semaphore_wait(barrier, n)
-
-    def transfer(packed, landing, which, step):
-        dest = lax.rem(me + step, n)
+    below_me = (plane + PLANES - 1) // PLANES
+    above_me = (2 * PLANES - 2 - plane) // PLANES
+    pl.semaphore_wait(barrier, width + below_me + above_me)
+
+    hops = PLANES - 1
+    origin = ((sorted_k, sorted_v), (send_k, send_v), (recv_k, recv_v))
+
+    def landing(which, way, hop):
+        return passing[(which * 2 + way) * hops + hop - 1]
+
+    def line(which, way, hop):
         return pltpu.make_async_remote_copy(
-            src_ref=packed.at[pl.ds(pl.multiple_of(dest * block, block), block)],
-            dst_ref=landing.at[pl.ds(pl.multiple_of(me * block, block), block)],
-            send_sem=send_sem.at[which, step],
-            recv_sem=recv_sem.at[which, step],
-            device_id={"blk": dest},
+            src_ref=origin[0][which] if hop == 1 else landing(which, way, hop - 1),
+            dst_ref=landing(which, way, hop),
+            send_sem=line_send.at[which, way, hop - 1],
+            recv_sem=line_recv.at[which, way, hop - 1],
+            device_id={"blk": me + (width if way == 0 else -width)},
             device_id_type=MESH,
         )
 
-    def start_k(step, carry):
-        transfer(send_k, recv_k, 0, step).start()
-        return carry
-
-    def start_v(step, carry):
-        transfer(send_v, recv_v, 1, step).start()
-        return carry
-
-    lax.fori_loop(1, n, start_k, 0)
-    lax.fori_loop(1, n, start_v, 0)
-    mine = pl.ds(pl.multiple_of(me * block, block), block)
-    recv_k[mine, :] = send_k[mine, :]
-    recv_v[mine, :] = send_v[mine, :]
+    def source_plane(way, hop):
+        return plane - hop if way == 0 else plane + hop
+
+    def arrives(way, hop):
+        return plane >= hop if way == 0 else plane + hop < PLANES
+
+    def departs(way, hop):
+        if way == 0:
+            return jnp.logical_and(plane >= hop - 1, plane < PLANES - 1)
+        return jnp.logical_and(plane + hop - 1 < PLANES, plane > 0)
+
+    def deal(which, event, step):
+        slot = event * width + step
+        return pltpu.make_async_remote_copy(
+            src_ref=origin[1][which].at[slot],
+            dst_ref=origin[2][which].at[event, pl.ds(pl.multiple_of(column * block, block), block)],
+            send_sem=send_sem.at[which, slot],
+            recv_sem=recv_sem.at[which, slot],
+            device_id={"blk": in_plane(step)},
+            device_id_type=MESH,
+        )
+
+    def deal_all(which, event, held):
+        def one(step, carry):
+            origin[1][which][event * width + step] = held[asked_ref[in_plane(step)]]
+            deal(which, event, step).start()
+            return carry
+
+        lax.fori_loop(1, width, one, 0)
+        origin[2][which][event, pl.ds(pl.multiple_of(column * block, block), block), :] = held[
+            asked_ref[me]
+        ]
+
+    def event_of(way, hop):
+        return 1 + way * hops + hop - 1
+
+    def send_line(which, way, hop):
+        @pl.when(departs(way, hop))
+        def _():
+            line(which, way, hop).start()
+
+    def handle(way, hop):
+        @pl.when(arrives(way, hop))
+        def _():
+            for which in range(2):
+                line(which, way, hop).wait_recv()
+                if hop < hops:
+                    send_line(which, way, hop + 1)
+                deal_all(which, event_of(way, hop), landing(which, way, hop))
+
+    for which in range(2):
+        for way in range(2):
+            send_line(which, way, 1)
+    for which in range(2):
+        deal_all(which, 0, origin[0][which])
 
     my_query = asked_ref[me]
     wanted = jnp.sum(
@@ -196,6 +256,8 @@
     )
     allowed_token = place_id * page + iota((1, tokens), 1) % page < length_ref[my_query]
     bias = jnp.where(allowed_token, 0.0, NEG).astype(F32)
+    for index in range(PLANES):
+        bias_ref[index] = bias[:, index * local : (index + 1) * local]
 
     buckets = embed_ref.shape[0]
     distances = bucket_ref.shape[1]
@@ -225,6 +287,7 @@
         tile, tile_rows, pair_cols = place(step)
         q = q_ref[tile_rows, pair_cols]
         k = k_ref[tile_rows, pair_cols]
+        v = v_ref[tile_rows, pair_cols]
         kr = key_rel[:, pair_cols]
         qr = query_rel[:, pair_cols]
         allowed = jnp.where(same_short, 1, kind_ref[tile]) == 1
@@ -232,64 +295,72 @@
             qh = jnp.where(halves[half], q, jnp.zeros_like(q))
             kh = jnp.where(halves[half], k, jnp.zeros_like(k))
             scores = dot_t(qh, k) + skew(dot_t(qh, kr)) + skew(dot_t(kh, qr)).T
-            own[step * 2 + half] = jnp.where(allowed, scores, NEG)
+            scores = jnp.where(allowed, scores, NEG)
+            top = jnp.max(scores, axis=1, keepdims=True)
+            weights = jnp.exp2((scores - top) * factor).astype(BF16)
+            top_ref[step * 2 + half] = top
+            acc[step * 2 + half] = jnp.dot(
+                weights,
+                jnp.where(halves[half], v, jnp.ones_like(v)),
+                preferred_element_type=F32,
+            )
         return carry
 
     for load in loads[3:]:
         load.wait()
     lax.fori_loop(0, tiles * pairs, own_scores, 0)
 
-    def land_k(step, carry):
-        transfer(send_k, recv_k, 0, step).wait_recv()
-        return carry
-
-    lax.fori_loop(1, n, land_k, 0)
-
-    def weigh(step, carry):
-        tile, tile_rows, pair_cols = place(step)
-        q = q_ref[tile_rows, pair_cols]
-        keys = recv_k[:, pair_cols]
-        for half in range(2):
-            qh = jnp.where(halves[half], q, jnp.zeros_like(q))
-            cross = dot_t(qh, keys) + bias
-            inner = own[step * 2 + half]
-            top = jnp.maximum(
-                jnp.max(cross, axis=1, keepdims=True), jnp.max(inner, axis=1, keepdims=True)
+    def absorb(event, chunk):
+        for which in range(2):
+            lax.fori_loop(
+                1, width, lambda step, carry: (deal(which, event, step).wait_recv(), carry)[1], 0
             )
-            probs[step * 2 + half, :, :tokens] = jnp.exp2((cross - top) * factor).astype(BF16)
-            probs[step * 2 + half, :, tokens:] = jnp.exp2((inner - top) * factor).astype(BF16)
-        return carry
-
-    lax.fori_loop(0, tiles * pairs, weigh, 0)
-
-    def land_v(step, carry):
-        transfer(send_v, recv_v, 1, step).wait_recv()
-        return carry
-
-    lax.fori_loop(1, n, land_v, 0)
-
-    def gather_values(step, carry):
-        tile, tile_rows, pair_cols = place(step)
-        values = recv_v[:, pair_cols]
-        inner = v_ref[tile_rows, pair_cols]
-        sums = []
-        for half in range(2):
-            weights = probs[step * 2 + half]
-            sums.append(
-                jnp.dot(
-                    weights[:, :tokens],
+        offset = bias_ref[chunk]
+
+        def update(step, carry):
+            tile, tile_rows, pair_cols = place(step)
+            q = q_ref[tile_rows, pair_cols]
+            keys = recv_k[event, :, pair_cols]
+            values = recv_v[event, :, pair_cols]
+            for half in range(2):
+                qh = jnp.where(halves[half], q, jnp.zeros_like(q))
+                scores = dot_t(qh, keys) + offset
+                before = top_ref[step * 2 + half]
+                top = jnp.maximum(before, jnp.max(scores, axis=1, keepdims=True))
+                weights = jnp.exp2((scores - top) * factor).astype(BF16)
+                top_ref[step * 2 + half] = top
+                acc[step * 2 + half] = acc[step * 2 + half] * jnp.exp2(
+                    (before - top) * factor
+                ) + jnp.dot(
+                    weights,
                     jnp.where(halves[half], values, jnp.ones_like(values)),
                     preferred_element_type=F32,
                 )
-                + jnp.dot(
-                    weights[:, tokens:],
-                    jnp.where(halves[half], inner, jnp.ones_like(inner)),
-                    preferred_element_type=F32,
-                )
-            )
-        top = jnp.where(halves[0], sums[0], sums[1])
+            return carry
+
+        lax.fori_loop(0, tiles * pairs, update, 0)
+
+    def absorb_event(way, hop):
+        @pl.when(arrives(way, hop))
+        def _():
+            absorb(event_of(way, hop), source_plane(way, hop))
+
+    handle(0, 1)
+    handle(1, 1)
+    absorb(0, plane)
+    for hop in range(1, hops + 1):
+        for way in range(2):
+            absorb_event(way, hop)
+        if hop < hops:
+            for way in range(2):
+                handle(way, hop + 1)
+
+    def finish(step, carry):
+        tile, tile_rows, pair_cols = place(step)
+        sums = [acc[step * 2], acc[step * 2 + 1]]
+        above = jnp.where(halves[0], sums[0], sums[1])
         below = pltpu.roll(jnp.where(halves[0], sums[1], sums[0]), HD, 1)
-        att[tile_rows, pair_cols] = (top / below).astype(BF16)
+        att[tile_rows, pair_cols] = (above / below).astype(BF16)
         return carry
 
     def swap(tile):
@@ -303,7 +374,7 @@
         )
 
     for tile in range(tiles):
-        lax.fori_loop(tile * pairs, (tile + 1) * pairs, gather_values, 0)
+        lax.fori_loop(tile * pairs, (tile + 1) * pairs, finish, 0)
         part[tile] = jnp.dot(
             att[tile * DOCLEN : (tile + 1) * DOCLEN, :], ow_ref[...], preferred_element_type=F32
         ).astype(BF16)
@@ -330,17 +401,30 @@
         full = firsts * gain_ref[...] + lnb_ref[...]
         scores = jnp.sum(full * sw_ref[...], axis=1, keepdims=True)
         segments = DOCLEN // SHORT
-        column = iota((segments, tiles * segments), 1) - tile * segments
-        spread_scores = jnp.where(iota((segments, tiles * segments), 0) == column, scores, 0.0)
+        lane_id = iota((segments, tiles * segments), 1) - tile * segments
+        spread_scores = jnp.where(iota((segments, tiles * segments), 0) == lane_id, scores, 0.0)
         seg_row = seg_row + jnp.sum(spread_scores, axis=0, keepdims=True)
     seg_ref[...] = seg_row
 
-    def drain(step, carry):
-        transfer(send_k, recv_k, 0, step).wait_send()
-        transfer(send_v, recv_v, 1, step).wait_send()
-        return carry
-
-    lax.fori_loop(1, n, drain, 0)
+    def drain(event):
+        for which in range(2):
+            lax.fori_loop(
+                1, width, lambda step, carry: (deal(which, event, step).wait_send(), carry)[1], 0
+            )
+
+    drain(0)
+    for way in range(2):
+        for hop in range(1, hops + 1):
+
+            @pl.when(departs(way, hop))
+            def _():
+                for which in range(2):
+                    line(which, way, hop).wait_send()
+
+            @pl.when(arrives(way, hop))
+            def _():
+                drain(event_of(way, hop))
+
     for tile in range(tiles):
         swap(tile).wait_send()
 
@@ -371,6 +455,8 @@
     tokens = query_pages * page
     block = pages_here // queries * page
     rows, model = doc_x.shape
+    width = n // PLANES
+    events = 2 * PLANES - 1
     tiles = rows // DOCLEN
     heads_here = cols // HD
 
@@ -395,24 +481,28 @@
             pltpu.VMEM((rows, model), BF16),
             pltpu.VMEM((queries, block, cols), BF16),
             pltpu.VMEM((queries, block, cols), BF16),
-            pltpu.VMEM((n * block, cols), BF16),
-            pltpu.VMEM((n * block, cols), BF16),
-            pltpu.VMEM((tokens, cols), BF16),
-            pltpu.VMEM((tokens, cols), BF16),
+            pltpu.VMEM((events * width, block, cols), BF16),
+            pltpu.VMEM((events * width, block, cols), BF16),
+            pltpu.VMEM((events, width * block, cols), BF16),
+            pltpu.VMEM((events, width * block, cols), BF16),
             pltpu.VMEM((2 * DOCLEN, cols), BF16),
             pltpu.VMEM((2 * DOCLEN, cols), BF16),
-            pltpu.VMEM((tiles * heads_here, DOCLEN, DOCLEN), F32),
-            pltpu.VMEM((tiles * heads_here, DOCLEN, tokens + DOCLEN), BF16),
+            pltpu.VMEM((PLANES, 1, tokens // PLANES), F32),
+            pltpu.VMEM((tiles * heads_here, DOCLEN, 1), F32),
+            pltpu.VMEM((tiles * heads_here, DOCLEN, 2 * HD), F32),
             pltpu.VMEM((rows, cols), BF16),
             pltpu.VMEM((tiles, DOCLEN, model), BF16),
             pltpu.VMEM((tiles, DOCLEN, model), BF16),
             pltpu.VMEM((DOCLEN, model), F32),
             pltpu.SemaphoreType.DMA((8,)),
-            pltpu.SemaphoreType.DMA((2, n)),
-            pltpu.SemaphoreType.DMA((2, n)),
+            pltpu.SemaphoreType.DMA((2, 2, PLANES - 1)),
+            pltpu.SemaphoreType.DMA((2, 2, PLANES - 1)),
+            pltpu.SemaphoreType.DMA((2, events * width)),
+            pltpu.SemaphoreType.DMA((2, events * width)),
             pltpu.SemaphoreType.DMA((tiles,)),
             pltpu.SemaphoreType.DMA((tiles,)),
-        ],
+        ]
+        + [pltpu.VMEM((queries, block, cols), BF16)] * (4 * (PLANES - 1)),
         compiler_params=pltpu.CompilerParams(
             collective_id=0, has_side_effects=True, vmem_limit_bytes=56 * 1024 * 1024
         ),

time: 65.2 us -> 75.9 us (1.16)
  the two profiles are of different devices: /device:TPU:15 before, /device:TPU:1 now
where the time goes in v2:
time: 75.9 us; the launch traced here: 75.7 us
  Pallas kernels  72.7 us (96%)
  local copies, waits for them, and re-layouts  2.38 us (3%)
    pallas_call x1, Pallas kernels, shards(): pl.pallas_call(functools.partial(kernel, n), out_shape=(jax.ShapeDtypeStr...  72.7 us
    unnamed x4, local copies, waits for them, and re-layouts  2.38 us

profile of v2, /device:TPU:1, one launch (start us, length us, event | category | flops | bytes accessed | tf_op | source)
XLA Modules:
  0.0 75.7 jit_solution(13672322096837667927)
XLA Ops:
  0.6 72.7 %shard_map.185 = (bf16[512,512]{1,0:T(8,128)(2,1)}, f32[1,32]{1,0:T(1,128)}) custom-call(s32[2]{0:T(128)} %kind_ref.1, s32[16]{0:T(128)} %asked_ref.1, s32[4]{0:T(128)} %length_ref.1, s32[4,64]{1,0:T(4,128)} %table_ref.1, bf16[16,16,512]{2,1,0:T(8,128)(2,1)} %keyc_ref.1, bf16[16,16,512]{2,1,0:T(8,128)(2,1)} %valuec_ref.1, s32[1,511]{1,0:T(1,128)} %bitcast.8, ...), custom_call_target="tpu_custom_call" | custom-call | flops 8000000000 | bytes 12000000 | tf_op jit(solution)/shard_map/pallas_call | solution.py:465
  73.3 0.0 copy-start
  73.3 1.9 %copy.22 = bf16[512,512]{1,0:T(8,128)(2,1)} copy(bf16[512,512]{1,0:T(8,128)(2,1)} %get-tuple-element.8) | data formatting | bytes 1048576
  75.2 0.0 copy-done
  75.2 0.5 copy.23
Async XLA Ops:
  73.3 1.9 %copy-start = (f32[1,32]{1,0:T(1,128)S(1)}, f32[1,32]{1,0:T(1,128)}, u32[]{:S(2)}) copy-start(f32[1,32]{1,0:T(1,128)} %get-tuple-element.5) | copy-start | bytes 388

commit v3 on v2

--- a/solution.py
+++ b/solution.py
@@ -277,38 +277,46 @@
         == lax.broadcasted_iota(jnp.int32, (DOCLEN, DOCLEN), 1) // SHORT
     )
 
-    def place(step):
-        tile, pair = step // pairs, step % pairs
-        tile_rows = pl.ds(pl.multiple_of(tile * DOCLEN, DOCLEN), DOCLEN)
-        pair_cols = pl.ds(pl.multiple_of(pair * 2 * HD, 2 * HD), 2 * HD)
-        return tile, tile_rows, pair_cols
-
-    def own_scores(step, carry):
-        tile, tile_rows, pair_cols = place(step)
-        q = q_ref[tile_rows, pair_cols]
-        k = k_ref[tile_rows, pair_cols]
-        v = v_ref[tile_rows, pair_cols]
+    def pair_span(pair):
+        return pl.ds(pl.multiple_of(pair * 2 * HD, 2 * HD), 2 * HD)
+
+    def tile_span(tile):
+        return slice(tile * DOCLEN, (tile + 1) * DOCLEN)
+
+    def own_scores(pair, carry):
+        pair_cols = pair_span(pair)
         kr = key_rel[:, pair_cols]
         qr = query_rel[:, pair_cols]
-        allowed = jnp.where(same_short, 1, kind_ref[tile]) == 1
-        for half in range(2):
-            qh = jnp.where(halves[half], q, jnp.zeros_like(q))
-            kh = jnp.where(halves[half], k, jnp.zeros_like(k))
-            scores = dot_t(qh, k) + skew(dot_t(qh, kr)) + skew(dot_t(kh, qr)).T
-            scores = jnp.where(allowed, scores, NEG)
-            top = jnp.max(scores, axis=1, keepdims=True)
-            weights = jnp.exp2((scores - top) * factor).astype(BF16)
-            top_ref[step * 2 + half] = top
-            acc[step * 2 + half] = jnp.dot(
-                weights,
-                jnp.where(halves[half], v, jnp.ones_like(v)),
-                preferred_element_type=F32,
-            )
+        results = []
+        for tile in range(tiles):
+            q = q_ref[tile_span(tile), pair_cols]
+            k = k_ref[tile_span(tile), pair_cols]
+            v = v_ref[tile_span(tile), pair_cols]
+            allowed = jnp.where(same_short, 1, kind_ref[tile]) == 1
+            for half in range(2):
+                qh = jnp.where(halves[half], q, jnp.zeros_like(q))
+                kh = jnp.where(halves[half], k, jnp.zeros_like(k))
+                scores = dot_t(qh, k) + skew(dot_t(qh, kr)) + skew(dot_t(kh, qr)).T
+                scores = jnp.where(allowed, scores, NEG)
+                top = jnp.max(scores, axis=1, keepdims=True)
+                weights = jnp.exp2((scores - top) * factor).astype(BF16)
+                total = jnp.dot(
+                    weights,
+                    jnp.where(halves[half], v, jnp.ones_like(v)),
+                    preferred_element_type=F32,
+                )
+                results.append((tile, half, top, total))
+        for tile, half, top, total in results:
+            top_ref[pair * 2 + half, tile_span(tile), :] = top
+            acc[pair * 2 + half, tile_span(tile), :] = total
         return carry
 
     for load in loads[3:]:
         load.wait()
-    lax.fori_loop(0, tiles * pairs, own_scores, 0)
+    lax.fori_loop(0, pairs // 2, own_scores, 0)
+    handle(0, 1)
+    handle(1, 1)
+    lax.fori_loop(pairs // 2, pairs, own_scores, 0)
 
     def absorb(event, chunk):
         for which in range(2):
@@ -318,50 +326,52 @@
         offset = bias_ref[chunk]
 
         def update(step, carry):
-            tile, tile_rows, pair_cols = place(step)
-            q = q_ref[tile_rows, pair_cols]
-            keys = recv_k[event, :, pair_cols]
-            values = recv_v[event, :, pair_cols]
-            for half in range(2):
-                qh = jnp.where(halves[half], q, jnp.zeros_like(q))
-                scores = dot_t(qh, keys) + offset
-                before = top_ref[step * 2 + half]
-                top = jnp.maximum(before, jnp.max(scores, axis=1, keepdims=True))
-                weights = jnp.exp2((scores - top) * factor).astype(BF16)
-                top_ref[step * 2 + half] = top
-                acc[step * 2 + half] = acc[step * 2 + half] * jnp.exp2(
-                    (before - top) * factor
-                ) + jnp.dot(
-                    weights,
-                    jnp.where(halves[half], values, jnp.ones_like(values)),
-                    preferred_element_type=F32,
-                )
+            results = []
+            for pair in (step * 2, step * 2 + 1):
+                pair_cols = pair_span(pair)
+                q = q_ref[:, pair_cols]
+                keys = recv_k[event, :, pair_cols]
+                values = recv_v[event, :, pair_cols]
+                for half in range(2):
+                    qh = jnp.where(halves[half], q, jnp.zeros_like(q))
+                    scores = dot_t(qh, keys) + offset
+                    before = top_ref[pair * 2 + half]
+                    top = jnp.maximum(before, jnp.max(scores, axis=1, keepdims=True))
+                    weights = jnp.exp2((scores - top) * factor).astype(BF16)
+                    total = acc[pair * 2 + half] * jnp.exp2((before - top) * factor) + jnp.dot(
+                        weights,
+                        jnp.where(halves[half], values, jnp.ones_like(values)),
+                        preferred_element_type=F32,
+                    )
+                    results.append((pair * 2 + half, top, total))
+            for index, top, total in results:
+                top_ref[index] = top
+                acc[index] = total
             return carry
 
-        lax.fori_loop(0, tiles * pairs, update, 0)
+        lax.fori_loop(0, pairs // 2, update, 0)
 
     def absorb_event(way, hop):
         @pl.when(arrives(way, hop))
         def _():
             absorb(event_of(way, hop), source_plane(way, hop))
 
-    handle(0, 1)
-    handle(1, 1)
     absorb(0, plane)
     for hop in range(1, hops + 1):
-        for way in range(2):
-            absorb_event(way, hop)
         if hop < hops:
             for way in range(2):
                 handle(way, hop + 1)
-
-    def finish(step, carry):
-        tile, tile_rows, pair_cols = place(step)
-        sums = [acc[step * 2], acc[step * 2 + 1]]
-        above = jnp.where(halves[0], sums[0], sums[1])
-        below = pltpu.roll(jnp.where(halves[0], sums[1], sums[0]), HD, 1)
-        att[tile_rows, pair_cols] = (above / below).astype(BF16)
-        return carry
+        for way in range(2):
+            absorb_event(way, hop)
+
+    def finish(tile):
+        for pair in range(pairs):
+            sums = [acc[pair * 2 + half, tile_span(tile), :] for half in range(2)]
+            above = jnp.where(halves[0], sums[0], sums[1])
+            below = pltpu.roll(jnp.where(halves[0], sums[1], sums[0]), HD, 1)
+            att[tile_span(tile), pair * 2 * HD : (pair + 1) * 2 * HD] = (above / below).astype(
+                BF16
+            )
 
     def swap(tile):
         return pltpu.make_async_remote_copy(
@@ -374,7 +384,7 @@
         )
 
     for tile in range(tiles):
-        lax.fori_loop(tile * pairs, (tile + 1) * pairs, finish, 0)
+        finish(tile)
         part[tile] = jnp.dot(
             att[tile * DOCLEN : (tile + 1) * DOCLEN, :], ow_ref[...], preferred_element_type=F32
         ).astype(BF16)
@@ -488,8 +498,8 @@
             pltpu.VMEM((2 * DOCLEN, cols), BF16),
             pltpu.VMEM((2 * DOCLEN, cols), BF16),
             pltpu.VMEM((PLANES, 1, tokens // PLANES), F32),
-            pltpu.VMEM((tiles * heads_here, DOCLEN, 1), F32),
-            pltpu.VMEM((tiles * heads_here, DOCLEN, 2 * HD), F32),
+            pltpu.VMEM((heads_here, rows, 1), F32),
+            pltpu.VMEM((heads_here, rows, 2 * HD), F32),
             pltpu.VMEM((rows, cols), BF16),
             pltpu.VMEM((tiles, DOCLEN, model), BF16),
             pltpu.VMEM((tiles, DOCLEN, model), BF16),

time: 75.9 us -> 64 us (0.84)
  Pallas kernels: 72.7 us -> 60.8 us
    pallas_call x1, Pallas kernels: 72.7 us -> 60.8 us  [shards(): pl.pallas_call(functools.partial(kernel, n), out_shape=(jax.ShapeDtypeStr...]
where the time goes in v3:
time: 64 us; the launch traced here: 63.8 us
  Pallas kernels  60.8 us (95%)
  local copies, waits for them, and re-layouts  2.38 us (4%)
  between operations  0.66 us (1%)
    pallas_call x1, Pallas kernels, shards(): pl.pallas_call(functools.partial(kernel, n), out_shape=(jax.ShapeDtypeStr...  60.8 us
    unnamed x4, local copies, waits for them, and re-layouts  2.38 us

profile of v3, /device:TPU:1, one launch (start us, length us, event | category | flops | bytes accessed | tf_op | source)
XLA Modules:
  0.0 63.8 jit_solution(2967263976509706563)
XLA Ops:
  0.6 60.8 %shard_map.185 = (bf16[512,512]{1,0:T(8,128)(2,1)}, f32[1,32]{1,0:T(1,128)}) custom-call(s32[2]{0:T(128)} %kind_ref.1, s32[16]{0:T(128)} %asked_ref.1, s32[4]{0:T(128)} %length_ref.1, s32[4,64]{1,0:T(4,128)} %table_ref.1, bf16[16,16,512]{2,1,0:T(8,128)(2,1)} %keyc_ref.1, bf16[16,16,512]{2,1,0:T(8,128)(2,1)} %valuec_ref.1, s32[1,511]{1,0:T(1,128)} %bitcast.8, ...), custom_call_target="tpu_custom_call" | custom-call | flops 8000000000 | bytes 12000000 | tf_op jit(solution)/shard_map/pallas_call | solution.py:475
  61.4 0.0 copy-start
  61.5 1.9 %copy.22 = bf16[512,512]{1,0:T(8,128)(2,1)} copy(bf16[512,512]{1,0:T(8,128)(2,1)} %get-tuple-element.8) | data formatting | bytes 1048576
  63.3 0.0 copy-done
  63.3 0.5 copy.23
Async XLA Ops:
  61.4 1.9 %copy-start = (f32[1,32]{1,0:T(1,128)S(1)}, f32[1,32]{1,0:T(1,128)}, u32[]{:S(2)}) copy-start(f32[1,32]{1,0:T(1,128)} %get-tuple-element.5) | copy-start | bytes 388

commit v4 on v3

--- a/solution.py
+++ b/solution.py
@@ -66,6 +66,7 @@
     bias_ref,
     top_ref,
     acc,
+    probs,
     att,
     part,
     other,
@@ -226,10 +227,10 @@
         def _():
             line(which, way, hop).start()
 
-    def handle(way, hop):
+    def handle(way, hop, kinds=(0, 1)):
         @pl.when(arrives(way, hop))
         def _():
-            for which in range(2):
+            for which in kinds:
                 line(which, way, hop).wait_recv()
                 if hop < hops:
                     send_line(which, way, hop + 1)
@@ -351,18 +352,78 @@
 
         lax.fori_loop(0, pairs // 2, update, 0)
 
+    def landed(which, event):
+        lax.fori_loop(
+            1, width, lambda step, carry: (deal(which, event, step).wait_recv(), carry)[1], 0
+        )
+
+    def weigh_last(event, chunk):
+        landed(0, event)
+        offset = bias_ref[chunk]
+
+        def update(step, carry):
+            results = []
+            for pair in (step * 2, step * 2 + 1):
+                pair_cols = pair_span(pair)
+                q = q_ref[:, pair_cols]
+                keys = recv_k[event, :, pair_cols]
+                for half in range(2):
+                    qh = jnp.where(halves[half], q, jnp.zeros_like(q))
+                    scores = dot_t(qh, keys) + offset
+                    before = top_ref[pair * 2 + half]
+                    top = jnp.maximum(before, jnp.max(scores, axis=1, keepdims=True))
+                    weights = jnp.exp2((scores - top) * factor).astype(BF16)
+                    total = acc[pair * 2 + half] * jnp.exp2((before - top) * factor)
+                    results.append((pair * 2 + half, weights, total))
+            for index, weights, total in results:
+                probs[index] = weights
+                acc[index] = total
+            return carry
+
+        lax.fori_loop(0, pairs // 2, update, 0)
+
+    def add_last(event):
+        landed(1, event)
+
+        def update(step, carry):
+            results = []
+            for pair in (step * 2, step * 2 + 1):
+                values = recv_v[event, :, pair_span(pair)]
+                for half in range(2):
+                    total = acc[pair * 2 + half] + jnp.dot(
+                        probs[pair * 2 + half],
+                        jnp.where(halves[half], values, jnp.ones_like(values)),
+                        preferred_element_type=F32,
+                    )
+                    results.append((pair * 2 + half, total))
+            for index, total in results:
+                acc[index] = total
+            return carry
+
+        lax.fori_loop(0, pairs // 2, update, 0)
+
     def absorb_event(way, hop):
         @pl.when(arrives(way, hop))
         def _():
             absorb(event_of(way, hop), source_plane(way, hop))
 
     absorb(0, plane)
-    for hop in range(1, hops + 1):
-        if hop < hops:
-            for way in range(2):
-                handle(way, hop + 1)
+    for hop in range(1, hops):
+        for way in range(2):
+            handle(way, hop + 1, (0, 1) if hop + 1 < hops else (0,))
         for way in range(2):
             absorb_event(way, hop)
+    for way in range(2):
+
+        @pl.when(arrives(way, hops))
+        def _():
+            weigh_last(event_of(way, hops), source_plane(way, hops))
+
+        handle(way, hops, (1,))
+
+        @pl.when(arrives(way, hops))
+        def _():
+            add_last(event_of(way, hops))
 
     def finish(tile):
         for pair in range(pairs):
@@ -500,6 +561,7 @@
             pltpu.VMEM((PLANES, 1, tokens // PLANES), F32),
             pltpu.VMEM((heads_here, rows, 1), F32),
             pltpu.VMEM((heads_here, rows, 2 * HD), F32),
+            pltpu.VMEM((heads_here, rows, tokens // PLANES), BF16),
             pltpu.VMEM((rows, cols), BF16),
             pltpu.VMEM((tiles, DOCLEN, model), BF16),
             pltpu.VMEM((tiles, DOCLEN, model), BF16),

time: 64 us -> 62.5 us (0.977)
  Pallas kernels: 60.8 us -> 59.3 us
    pallas_call x1, Pallas kernels: 60.8 us -> 59.3 us  [shards(): pl.pallas_call(functools.partial(kernel, n), out_shape=(jax.ShapeDtypeStr...]
where the time goes in v4:
time: 62.5 us; the launch traced here: 62.4 us
  Pallas kernels  59.3 us (95%)
  local copies, waits for them, and re-layouts  2.38 us (4%)
  between operations  0.66 us (1%)
    pallas_call x1, Pallas kernels, shards(): pl.pallas_call(functools.partial(kernel, n), out_shape=(jax.ShapeDtypeStr...  59.3 us
    unnamed x4, local copies, waits for them, and re-layouts  2.38 us

profile of v4, /device:TPU:1, one launch (start us, length us, event | category | flops | bytes accessed | tf_op | source)
XLA Modules:
  0.0 62.4 jit_solution(11052370688877391211)
XLA Ops:
  0.6 59.3 %shard_map.185 = (bf16[512,512]{1,0:T(8,128)(2,1)}, f32[1,32]{1,0:T(1,128)}) custom-call(s32[2]{0:T(128)} %kind_ref.1, s32[16]{0:T(128)} %asked_ref.1, s32[4]{0:T(128)} %length_ref.1, s32[4,64]{1,0:T(4,128)} %table_ref.1, bf16[16,16,512]{2,1,0:T(8,128)(2,1)} %keyc_ref.1, bf16[16,16,512]{2,1,0:T(8,128)(2,1)} %valuec_ref.1, s32[1,511]{1,0:T(1,128)} %bitcast.8, ...), custom_call_target="tpu_custom_call" | custom-call | flops 8000000000 | bytes 12000000 | tf_op jit(solution)/shard_map/pallas_call | solution.py:536
  60.0 0.0 copy-start
  60.0 1.9 %copy.22 = bf16[512,512]{1,0:T(8,128)(2,1)} copy(bf16[512,512]{1,0:T(8,128)(2,1)} %get-tuple-element.8) | data formatting | bytes 1048576
  61.9 0.0 copy-done
  61.9 0.5 copy.23
Async XLA Ops:
  60.0 1.9 %copy-start = (f32[1,32]{1,0:T(1,128)S(1)}, f32[1,32]{1,0:T(1,128)}, u32[]{:S(2)}) copy-start(f32[1,32]{1,0:T(1,128)} %get-tuple-element.5) | copy-start | bytes 388
